TPU v7x, 32 devices: a whole 2x2x4 slice. The times are simulated.
32 devices in a mesh: cin: 8 (over z, x), cout: 2 (over y), depth: 2 (over core).
Axes of the slice: x: 2, y: 2, z: 4, core: 2. Of those that a mesh axis runs over, the one named last changes fastest.
Arguments:
- features: bfloat16 [8, 512, 4, 128], P(None, 'cin', 'depth'), may hold values from -6 to 6
- kernel: bfloat16 [27, 512, 512], P(None, 'cout', 'cin'), may hold values from -0.0546875 to 0.0546875
- grad_out: bfloat16 [8, 512, 4, 128], P('cin', 'cout', 'depth'), may hold values from -6 to 6
Outputs:
- output: bfloat16 [8, 512, 4, 128], P('cin', 'cout', 'depth')
- input_grad: bfloat16 [8, 512, 4, 128], P('cout', 'cin', 'depth')
- kernel_grad: float32 [27, 512, 512], P(None, 'cout', 'cin')
All inputs are finite; a program needn't handle non-finite values.
Results may differ from a plain program's by a relative error of at most 0.001.
Values may be sent and summed in bfloat16 or wider, within the bound.
No kernel may reach another device: no remote copies, remote signals or barrier semaphores. Data moves between devices by JAX's collectives and lax.ppermute only.
A program may use at most 128 MiB of HBM per device.

v0:
```python
import math
import jax
import jax.numpy as jnp
from jax import lax
from jax.sharding import PartitionSpec as P


def padded_2(x, sides, width):
    for axis, dim in sides:
        size, length = (lax.axis_size(axis), x.shape[dim])
        up = [(i, (i + 1) % size) for i in range(size - 1)]
        down = [(j, i) for i, j in up]
        last = lax.slice_in_dim(x, length - width, length, axis=dim)
        first = lax.slice_in_dim(x, 0, width, axis=dim)
        before = lax.ppermute(last, axis, up)
        after = lax.ppermute(first, axis, down)
        x = jnp.concatenate([before, x, after], axis=dim)
    return x


def conv_rows(padded, weight, count, slab, width):
    total = None
    for depth_off in range(3):
        pieces = [
            padded[
                row_off : row_off + count,
                :,
                depth_off : depth_off + slab,
                col_off : col_off + width,
            ]
            for row_off in range(3)
            for col_off in range(3)
        ]
        stacked = jnp.stack(pieces, axis=1)
        term = jnp.einsum(
            "toc,htcdw->hodw",
            weight[9 * depth_off : 9 * depth_off + 9],
            stacked,
            preferred_element_type=jnp.float32,
        )
        total = term if total is None else total + term
    return total


def weight_terms(padded, grad_own, count, slab, width):
    parts = []
    for depth_off in range(3):
        pieces = [
            padded[
                row_off : row_off + count,
                :,
                depth_off : depth_off + slab,
                col_off : col_off + width,
            ]
            for row_off in range(3)
            for col_off in range(3)
        ]
        stacked = jnp.stack(pieces, axis=1)
        parts.append(
            jnp.einsum("hodw,htcdw->toc", grad_own, stacked, preferred_element_type=jnp.float32)
        )
    return jnp.concatenate(parts, axis=0)


def per_device(features, kernel, grad_out):
    rows_all = features.shape[0]
    slab = features.shape[2]
    width = features.shape[3]
    chan_in = features.shape[1]
    rows_own = rows_all // lax.axis_size("cin")
    slab_ext = padded_2(features, (("depth", 2),), 1)
    feat_pad = jnp.pad(slab_ext, ((1, 1), (0, 0), (0, 0), (1, 1)))
    block = feat_pad
    output = lax.psum_scatter(
        conv_rows(block, kernel, lax.axis_size("cin") * rows_own, slab, width),
        "cin",
        scatter_dimension=0,
        tiled=True,
    ).astype(jnp.bfloat16)
    grad_full = lax.all_gather(grad_out, "cin", axis=0, tiled=True)
    grad_full = padded_2(grad_full, (("depth", 2),), 1)
    grad_pad = jnp.pad(grad_full, ((1, 1), (0, 0), (0, 0), (0, 0)))
    rows_grad = rows_all // lax.axis_size("cout")
    block = grad_pad
    total = jnp.zeros((lax.axis_size("cout") * rows_grad, chan_in, slab, width), jnp.float32)
    for depth_off in range(3):
        part = block[:, :, 2 - depth_off : 2 - depth_off + slab, :]
        mixed = jnp.einsum(
            "toc,hodw->thcdw",
            kernel[9 * depth_off : 9 * depth_off + 9],
            part,
            preferred_element_type=jnp.float32,
        )
        mixed = jnp.pad(mixed, ((0, 0), (0, 0), (0, 0), (0, 0), (1, 1)))
        for row_off in range(3):
            for col_off in range(3):
                total = (
                    total
                    + mixed[
                        3 * row_off + col_off,
                        2 - row_off : 2 - row_off + lax.axis_size("cout") * rows_grad,
                        :,
                        :,
                        2 - col_off : 2 - col_off + width,
                    ]
                )
    input_grad = lax.psum_scatter(total, "cout", scatter_dimension=0, tiled=True).astype(
        jnp.bfloat16
    )
    grad_own = grad_full[:, :, 1 : 1 + slab, :]
    local_terms = weight_terms(feat_pad, grad_own, rows_all, slab, width)
    summed = lax.psum(local_terms, "depth")
    cells = rows_all * slab * lax.axis_size("depth") * width
    kernel_grad = summed * (1.0 / math.sqrt(cells))
    return (output, input_grad, kernel_grad)


def solution(mesh):
    return jax.shard_map(
        per_device,
        mesh=mesh,
        in_specs=(
            P(None, "cin", "depth", None),
            P(None, "cout", "cin"),
            P("cin", "cout", "depth", None),
        ),
        out_specs=(
            P("cin", "cout", "depth", None),
            P("cout", "cin", "depth", None),
            P(None, "cout", "cin"),
        ),
        check_vma=False,
    )
```

profile of v0, /device:TPU:0, one launch (start us, length us, event | category | flops | bytes accessed | tf_op | source)
XLA Modules:
  0.0 189.4 jit_solution(8112478354780090528)
XLA Ops:
  7.2 1.0 copy.40
  8.2 2.4 %collective-permute-start = (bf16[8,64,1,128]{3,1,2,0:T(8,128)(2,1)S(1)}, bf16[8,64,1,128]{3,1,2,0:T(8,128)(2,1)S(1)}, u32[]{:S(2)}, u32[]{:S(2)}) collective-permute-start(bf16[8,64,1,128]{3,1,2,0:T(8,128)(2,1)S(1)} %get-tuple-element.25), channel_id=1, source_target_pairs={{0,1},{2,3},{4,5},{6,7},{8,9},{10,11},{12,13},{14,15},{16,17},{18,... | collective-permute-start | bytes 393224 | tf_op jit(solution)/shard_map/ppermute | solution.py:15
  10.6 1.3 collective-permute-start.1
  11.9 1.6 copy.55
  13.9 0.5 select_maximum_fusion
  14.4 0.7 fusion.85
  15.1 0.8 fusion.95
  15.9 0.9 fusion.94
  16.8 0.9 fusion.93
  17.6 0.8 fusion.92
  18.4 0.9 fusion.84
  19.3 1.0 fusion.83
  20.3 0.9 fusion.82
  21.2 0.8 fusion.91
  22.0 0.8 bitcast_dynamic-update-slice_fusion
  22.8 0.9 fusion.81
  23.7 0.7 fusion.73
  24.4 0.9 fusion.89
  25.2 0.8 fusion.88
  26.0 0.8 fusion.87
  26.9 0.9 fusion.80
  27.8 0.9 fusion.79
  28.7 28.0 %all-gather.2.cloned.1.call-done = bf16[8,256,2,128]{3,1,2,0:T(8,128)(2,1)} async-done(((bf16[1,256,2,128]{3,1,2,0:T(8,128)(2,1)}), bf16[8,256,2,128]{3,1,2,0:T(8,128)(2,1)}) %all-gather.2.cloned.1.call-update) | async-done | bytes 1048592 | tf_op jit(solution)/shard_map/all_gather | solution.py:80
  56.7 1.4 fusion.104
  58.0 1.3 collective-permute-start.2
  59.4 1.3 collective-permute-start.3
  60.7 0.9 fusion.86
  61.6 1.0 fusion.78
  62.6 0.8 fusion.68
  63.8 0.8 copy-done.1
  64.6 0.9 convolution_bitcast_fusion.1
  65.5 0.9 convolution_bitcast_fusion.2
  66.5 0.9 convolution_bitcast_fusion
  67.4 3.3 %fusion.54 = f32[8,64,2,128]{3,1,2,0:T(8,128)} fusion(f32[9,10,64,2,128]{4,2,3,1,0:T(8,128)S(1)} %convolution_bitcast_fusion, f32[9,10,64,2,128]{4,2,3,1,0:T(8,128)S(1)} %convolution_bitcast_fusion.1, f32[9,10,64,2,128]{4,2,0,3,1:T(8,128)S(1)} %convolution_bitcast_fusion.2), kind=kLoop, calls=%fused_computation.90 | loop fusion | flops 3407872 | bytes 22937600 | tf_op jit(solution)/shard_map/add | solution.py:98
  70.8 2.5 %convolution_bitcast_fusion.3 = f32[9,256,64]{1,2,0:T(8,128)S(1)} fusion(bf16[8,9,64,2,128]{4,2,3,0,1:T(8,128)(2,1)} %fusion.68, bf16[8,256,2,128]{3,1,2,0:T(8,128)(2,1)S(1)} %copy-done), kind=kOutput, calls=%fused_computation.55 | convolution fusion | flops 603979776 | bytes 3997696 | tf_op jit(solution)/shard_map/hodw,htcdw->toc/dot_general | solution.py:60
  73.3 2.5 %convolution_bitcast_fusion.4 = f32[9,256,64]{1,2,0:T(8,128)S(1)} fusion(bf16[8,9,64,2,128]{4,2,3,0,1:T(8,128)(2,1)} %get-tuple-element.9, bf16[8,256,2,128]{3,1,2,0:T(8,128)(2,1)S(1)} %copy-done), kind=kOutput, calls=%fused_computation.56 | convolution fusion | flops 603979776 | bytes 3997696 | tf_op jit(solution)/shard_map/hodw,htcdw->toc/dot_general | solution.py:60
  75.8 2.6 %fusion.19 = f32[9,256,64]{1,2,0:T(8,128)S(1)} fusion(bf16[8,9,64,2,128]{4,2,1,3,0:T(8,128)(2,1)} %fusion.86, bf16[8,256,2,128]{3,1,2,0:T(8,128)(2,1)S(1)} %copy-done), kind=kOutput, calls=%fused_computation.54 | convolution fusion | flops 603979776 | bytes 3997696 | tf_op jit(solution)/shard_map/hodw,htcdw->toc/dot_general | solution.py:60
  78.3 1.4 pad_maximum_fusion
  80.0 2.7 %fusion.13 = f32[8,2,128,256,1]{3,2,0,1,4:T(8,128)S(1)} fusion(bf16[8,9,64,2,128]{4,2,3,0,1:T(8,128)(2,1)} %get-tuple-element.9, bf16[27,256,64]{1,2,0:T(8,128)(2,1)S(1)} %copy-done.1), kind=kOutput, calls=%fused_computation.40 | convolution fusion | flops 603979776 | bytes 4751360 | tf_op jit(solution)/shard_map/toc,htcdw->hodw/dot_general | solution.py:35
  82.7 2.7 %fusion.11 = f32[8,2,128,256,1]{3,2,0,1,4:T(8,128)S(1)} fusion(bf16[8,9,64,2,128]{4,2,3,0,1:T(8,128)(2,1)} %fusion.68, bf16[27,256,64]{1,2,0:T(8,128)(2,1)S(1)} %copy-done.1), kind=kOutput, calls=%fused_computation.38 | convolution fusion | flops 603979776 | bytes 4751360 | tf_op jit(solution)/shard_map/toc,htcdw->hodw/dot_general | solution.py:35
  85.5 4.1 %fusion.15 = f32[8,256,2,128]{1,3,2,0:T(8,128)} fusion(f32[8,2,128,256,1]{3,2,0,1,4:T(8,128)S(1)} %fusion.11, f32[8,2,128,256,1]{3,2,0,1,4:T(8,128)S(1)} %fusion.13, bf16[8,9,64,2,128]{4,2,1,3,0:T(8,128)(2,1)} %fusion.86, bf16[27,256,64]{1,2,0:T(8,128)(2,1)S(1)} %copy-done.1), kind=kOutput, calls=%fused_computation.43 | convolution fusion | flops 605028352 | bytes 8945664 | tf_op jit(solution)/shard_map/toc,htcdw->hodw/dot_general | solution.py:35
  89.6 1.0 convert_element_type.15
  90.6 0.8 copy.73
  91.4 17.4 %all-reduce.7.cloned.1.call-done = f32[27,256,64]{1,2,0:T(8,128)} async-done(((f32[27,256,64]{1,2,0:T(8,128)}), f32[27,256,64]{1,2,0:T(8,128)}) %all-reduce.7.cloned.1.call-update) | async-done | bytes 1769488 | tf_op jit(solution)/shard_map/psum | solution.py:112
  108.8 2.9 %broadcast_multiply_fusion = f32[27,256,64]{1,2,0:T(8,128)} fusion(f32[27,256,64]{1,2,0:T(8,128)} %all-reduce.7.cloned.1.call-done), kind=kLoop, calls=%fused_computation.58 | loop fusion | flops 442368 | bytes 3538944 | tf_op jit(solution)/shard_map/mul | solution.py:114
  111.7 69.4 %reduce-scatter.3.cloned.1.call-done = f32[1,256,2,128]{1,3,2,0:T(8,128)} async-done(((f32[8,256,2,128]{1,3,2,0:T(8,128)}), f32[1,256,2,128]{1,3,2,0:T(8,128)}) %reduce-scatter.3.cloned.1.call-update) | async-done | bytes 262160 | tf_op jit(solution)/shard_map/reduce_scatter | solution.py:74
  181.1 1.0 convert_element_type.14
  182.1 0.8 copy.72
  (20 shorter events, 1.1 us)
Async XLA Ops:
  7.2 49.5 %all-gather.2.cloned.1.call-start = ((), (), s32[]{:S(2)}) async-start(), calls=%async_computation.3 | async-start | bytes 1179648 | tf_op jit(solution)/shard_map/all_gather | solution.py:80
  8.2 5.3 %collective-permute-start = (bf16[8,64,1,128]{3,1,2,0:T(8,128)(2,1)S(1)}, bf16[8,64,1,128]{3,1,2,0:T(8,128)(2,1)S(1)}, u32[]{:S(2)}, u32[]{:S(2)}) collective-permute-start(bf16[8,64,1,128]{3,1,2,0:T(8,128)(2,1)S(1)} %get-tuple-element.25), channel_id=1, source_target_pairs={{0,1},{2,3},{4,5},{6,7},{8,9},{10,11},{12,13},{14,15},{16,17},{18,... | collective-permute-start | bytes 393224 | tf_op jit(solution)/shard_map/ppermute | solution.py:15
  10.6 3.2 %collective-permute-start.1 = (bf16[8,64,1,128]{3,1,2,0:T(8,128)(2,1)S(1)}, bf16[8,64,1,128]{3,1,2,0:T(8,128)(2,1)S(1)}, u32[]{:S(2)}, u32[]{:S(2)}) collective-permute-start(bf16[8,64,1,128]{3,1,2,0:T(8,128)(2,1)S(1)} %get-tuple-element.26), channel_id=1, source_target_pairs={{1,0},{3,2},{5,4},{7,6},{9,8},{11,10},{13,12},{15,14},{17,16},{19,... | collective-permute-start | bytes 393224 | tf_op jit(solution)/shard_map/ppermute | solution.py:16
  13.5 76.1 %reduce-scatter.5.cloned.1.call-start = ((), (), s32[]{:S(2)}) async-start(), calls=%async_computation.4 | async-start | bytes 786432 | tf_op jit(solution)/shard_map/reduce_scatter | solution.py:107
  16.8 5.2 %copy-start.2 = (bf16[8,64,2,128]{3,2,1,0:T(2,128)(2,1)S(1)}, bf16[8,64,2,128]{3,2,1,0:T(2,128)(2,1)}, u32[]{:S(2)}) copy-start(bf16[8,64,2,128]{3,2,1,0:T(2,128)(2,1)} %param.3) | copy-start | bytes 786436
  56.7 6.8 %copy-start = (bf16[8,256,2,128]{3,1,2,0:T(8,128)(2,1)S(1)}, bf16[8,256,2,128]{3,1,2,0:T(8,128)(2,1)}, u32[]{:S(2)}) copy-start(bf16[8,256,2,128]{3,1,2,0:T(8,128)(2,1)} %all-gather.2.cloned.1.call-done) | copy-start | bytes 3145732
  58.0 5.4 %collective-permute-start.2 = (bf16[8,256,1,128]{3,1,2,0:T(8,128)(2,1)S(1)}, bf16[8,256,1,128]{3,1,2,0:T(8,128)(2,1)S(1)}, u32[]{:S(2)}, u32[]{:S(2)}) collective-permute-start(bf16[8,256,1,128]{3,1,2,0:T(8,128)(2,1)S(1)} %get-tuple-element.23), channel_id=1, source_target_pairs={{0,1},{2,3},{4,5},{6,7},{8,9},{10,11},{12,13},{14,15},{16,17},{18,... | collective-permute-start | bytes 1572872 | tf_op jit(solution)/shard_map/ppermute | solution.py:15
  59.4 4.1 %collective-permute-start.3 = (bf16[8,256,1,128]{3,1,2,0:T(8,128)(2,1)S(1)}, bf16[8,256,1,128]{3,1,2,0:T(8,128)(2,1)S(1)}, u32[]{:S(2)}, u32[]{:S(2)}) collective-permute-start(bf16[8,256,1,128]{3,1,2,0:T(8,128)(2,1)S(1)} %get-tuple-element.24), channel_id=1, source_target_pairs={{1,0},{3,2},{5,4},{7,6},{9,8},{11,10},{13,12},{15,14},{17,16},{19,... | collective-permute-start | bytes 1572872 | tf_op jit(solution)/shard_map/ppermute | solution.py:16
  63.4 1.2 copy-start.1
  70.8 38.1 %all-reduce.7.cloned.1.call-start = ((), (), s32[]{:S(2)}) async-start(), calls=%async_computation.5 | async-start | bytes 3538944 | tf_op jit(solution)/shard_map/psum | solution.py:112
  79.7 101.4 %reduce-scatter.3.cloned.1.call-start = ((), (), s32[]{:S(2)}) async-start(), calls=%async_computation.2 | async-start | bytes 2359296 | tf_op jit(solution)/shard_map/reduce_scatter | solution.py:74
Sparse Core Ops, SparseCore 0:
  13.6 42.9 all-gather.1
  70.9 14.0 reduce-scatter.4
  88.1 20.6 all-reduce.6
  112.2 68.8 reduce-scatter.2
where the time goes:
time: 190 us; the launch traced here: 189 us
  waiting for transfers between devices  115 us (61%)
  local copies, waits for them, and re-layouts  21.9 us (12%)
  matrix products  19.9 us (10%)
  between operations  13.9 us (7%)
  other arithmetic  11.9 us (6%)
  starting transfers between devices  6.61 us (3%)
    reduce_scatter x1, waiting for transfers between devices, per_device(): lax.psum_scatter(conv_rows(block, kernel, lax.axis_size('cin') * rows_own...  69.4 us
    all_gather x1, waiting for transfers between devices, per_device(): grad_full = lax.all_gather(grad_out, 'cin', axis=0, tiled=True)  28 us
    unnamed x25, local copies, waits for them, and re-layouts  17.7 us
    psum x1, waiting for transfers between devices, per_device(): summed = lax.psum(local_terms, 'depth')  17.4 us
    dot_general x3, matrix products, conv_rows(): jnp.einsum('toc,htcdw->hodw', weight[9 * depth_off:9 * depth_off + 9], st...  9.56 us
    dot_general x3, matrix products, weight_terms(): jnp.einsum('hodw,htcdw->toc', grad_own, stacked, preferred_element_type=j...  7.5 us
  transfers between devices with their start and end apart: 8, of which 4 were waited for; matrix products, arithmetic and copies ran while one was open for 22% of the time, Pallas kernels for 0%

commit v1 on v0

--- a/solution.py
+++ b/solution.py
@@ -3,6 +3,7 @@
 import jax.numpy as jnp
 from jax import lax
 from jax.sharding import PartitionSpec as P
+from jax.lax import all_gather
 
 
 def padded_2(x, sides, width):
@@ -109,7 +110,8 @@
     )
     grad_own = grad_full[:, :, 1 : 1 + slab, :]
     local_terms = weight_terms(feat_pad, grad_own, rows_all, slab, width)
-    summed = lax.psum(local_terms, "depth")
+    take_rows_here = lambda v0, axis_key: jnp.sum(all_gather(v0, axis_key), axis=0)
+    summed = take_rows_here(local_terms, "depth")
     cells = rows_all * slab * lax.axis_size("depth") * width
     kernel_grad = summed * (1.0 / math.sqrt(cells))
     return (output, input_grad, kernel_grad)

time: 190 us -> 182 us (0.958)
  waiting for transfers between devices: 115 us -> 106 us
    psum x1 -> x0, waiting for transfers between devices: 17.4 us -> none  [per_device(): summed = lax.psum(local_terms, 'depth')]
    all_gather x0 -> x1, waiting for transfers between devices: none -> 12 us  [per_device(): all_gather(v0, axis_key)]
    reduce_scatter x1, waiting for transfers between devices: 69.4 us -> 66.3 us  [per_device(): lax.psum_scatter(conv_rows(block, kernel, lax.axis_size('cin') * rows_own...]
    reduce_sum x0 -> x1, other arithmetic: none -> 2.46 us  [per_device(): jnp.sum(all_gather(v0, axis_key), axis=0)]
    unnamed x25 -> x27, local copies, waits for them, and re-layouts: 17.7 us -> 17.7 us
  transfers between devices with their start and end apart: 8 -> 8, of which waited for: 4 -> 4; matrix products, arithmetic and copies ran while one was open for 22% -> 23% of each run, Pallas kernels for 0% -> 0%
where the time goes in v1:
time: 182 us
  waiting for transfers between devices  106 us (58%)
  local copies, waits for them, and re-layouts  21.8 us (12%)
  matrix products  20.2 us (11%)
  between operations  14 us (8%)
  other arithmetic  12.8 us (7%)
  starting transfers between devices  6.61 us (4%)
    reduce_scatter x1, waiting for transfers between devices, per_device(): lax.psum_scatter(conv_rows(block, kernel, lax.axis_size('cin') * rows_own...  66.3 us
    all_gather x1, waiting for transfers between devices, per_device(): grad_full = lax.all_gather(grad_out, 'cin', axis=0, tiled=True)  27.8 us
    unnamed x27, local copies, waits for them, and re-layouts  17.7 us
    all_gather x1, waiting for transfers between devices, per_device(): all_gather(v0, axis_key)  12 us
    dot_general x3, matrix products, conv_rows(): jnp.einsum('toc,htcdw->hodw', weight[9 * depth_off:9 * depth_off + 9], st...  9.92 us
    dot_general x3, matrix products, weight_terms(): jnp.einsum('hodw,htcdw->toc', grad_own, stacked, preferred_element_type=j...  7.44 us
    ppermute x2, starting transfers between devices, padded_2(): before = lax.ppermute(last, axis, up)  3.69 us
  transfers between devices with their start and end apart: 8, of which 4 were waited for; matrix products, arithmetic and copies ran while one was open for 23% of the time, Pallas kernels for 0%

profile of v1, /device:TPU:0, one launch (start us, length us, event | category | flops | bytes accessed | tf_op | source)
XLA Modules:
  0.0 181.9 jit_solution(4241469650819792061)
XLA Ops:
  7.2 1.0 copy.40
  8.2 2.4 %collective-permute-start = (bf16[8,64,1,128]{3,1,2,0:T(8,128)(2,1)S(1)}, bf16[8,64,1,128]{3,1,2,0:T(8,128)(2,1)S(1)}, u32[]{:S(2)}, u32[]{:S(2)}) collective-permute-start(bf16[8,64,1,128]{3,1,2,0:T(8,128)(2,1)S(1)} %get-tuple-element.25), channel_id=1, source_target_pairs={{0,1},{2,3},{4,5},{6,7},{8,9},{10,11},{12,13},{14,15},{16,17},{18,... | collective-permute-start | bytes 393224 | tf_op jit(solution)/shard_map/ppermute | solution.py:16
  10.6 1.3 collective-permute-start.1
  11.9 1.6 copy.55
  14.4 0.8 fusion.85
  15.1 0.8 fusion.95
  15.9 0.9 fusion.94
  16.8 0.8 fusion.93
  17.6 0.8 fusion.92
  18.4 0.9 fusion.84
  19.3 1.0 fusion.83
  20.3 0.9 fusion.82
  21.2 0.8 fusion.91
  22.0 0.8 bitcast_dynamic-update-slice_fusion
  22.7 0.9 fusion.81
  23.6 0.7 fusion.73
  24.4 0.9 fusion.89
  25.2 0.8 fusion.88
  26.0 0.9 fusion.80
  26.9 0.9 fusion.79
  27.8 1.1 fusion.78
  28.9 27.8 %all-gather.4.cloned.1.call-done = bf16[8,256,2,128]{3,1,2,0:T(8,128)(2,1)} async-done(((bf16[1,256,2,128]{3,1,2,0:T(8,128)(2,1)}), bf16[8,256,2,128]{3,1,2,0:T(8,128)(2,1)}) %all-gather.4.cloned.1.call-update) | async-done | bytes 1048592 | tf_op jit(solution)/shard_map/all_gather | solution.py:81
  56.7 1.3 fusion.104
  58.0 1.3 collective-permute-start.2
  59.3 1.3 collective-permute-start.3
  60.6 0.9 fusion.87
  61.5 2.8 %fusion.13 = f32[8,2,128,256,1]{3,2,0,1,4:T(8,128)S(1)} fusion(bf16[8,9,64,2,128]{4,2,3,0,1:T(8,128)(2,1)} %get-tuple-element.9, bf16[27,256,64]{1,2,0:T(8,128)(2,1)} %param.4), kind=kOutput, calls=%fused_computation.40 | convolution fusion | flops 603979776 | bytes 4751360 | tf_op jit(solution)/shard_map/toc,htcdw->hodw/dot_general | solution.py:36
  64.7 0.8 copy-done.2
  65.5 0.9 convolution_bitcast_fusion.1
  66.4 0.9 convolution_bitcast_fusion.2
  67.3 0.9 convolution_bitcast_fusion
  68.3 3.3 %fusion.54 = f32[8,64,2,128]{3,1,2,0:T(8,128)} fusion(f32[9,10,64,2,128]{4,2,3,1,0:T(8,128)S(1)} %convolution_bitcast_fusion, f32[9,10,64,2,128]{4,2,3,1,0:T(8,128)S(1)} %convolution_bitcast_fusion.1, f32[9,10,64,2,128]{4,2,0,3,1:T(8,128)S(1)} %convolution_bitcast_fusion.2), kind=kLoop, calls=%fused_computation.90 | loop fusion | flops 3407872 | bytes 22937600 | tf_op jit(solution)/shard_map/add | solution.py:99
  71.8 0.9 fusion.86
  72.7 0.9 fusion.68
  73.6 2.7 %fusion.11 = f32[8,2,128,256,1]{3,2,0,1,4:T(8,128)S(1)} fusion(bf16[8,9,64,2,128]{4,2,3,0,1:T(8,128)(2,1)} %fusion.68, bf16[27,256,64]{1,2,0:T(8,128)(2,1)} %param.4), kind=kOutput, calls=%fused_computation.38 | convolution fusion | flops 603979776 | bytes 4751360 | tf_op jit(solution)/shard_map/toc,htcdw->hodw/dot_general | solution.py:36
  76.3 4.4 %fusion.15 = f32[8,256,2,128]{1,3,2,0:T(8,128)} fusion(f32[8,2,128,256,1]{3,2,0,1,4:T(8,128)S(1)} %fusion.11, f32[8,2,128,256,1]{3,2,0,1,4:T(8,128)S(1)} %fusion.13, bf16[8,9,64,2,128]{4,2,1,3,0:T(8,128)(2,1)} %fusion.86, bf16[27,256,64]{1,2,0:T(8,128)(2,1)} %param.4), kind=kOutput, calls=%fused_computation.43 | convolution fusion | flops 605028352 | bytes 8945664 | tf_op jit(solution)/shard_map/toc,htcdw->hodw/dot_general | solution.py:36
  80.8 2.5 %convolution_bitcast_fusion.3 = f32[9,256,64]{1,2,0:T(8,128)S(1)} fusion(bf16[8,9,64,2,128]{4,2,3,0,1:T(8,128)(2,1)} %fusion.68, bf16[8,256,2,128]{3,1,2,0:T(8,128)(2,1)S(1)} %copy-done.1), kind=kOutput, calls=%fused_computation.55 | convolution fusion | flops 603979776 | bytes 3997696 | tf_op jit(solution)/shard_map/hodw,htcdw->toc/dot_general | solution.py:61
  83.3 2.5 %convolution_bitcast_fusion.4 = f32[9,256,64]{1,2,0:T(8,128)S(1)} fusion(bf16[8,9,64,2,128]{4,2,3,0,1:T(8,128)(2,1)} %get-tuple-element.9, bf16[8,256,2,128]{3,1,2,0:T(8,128)(2,1)S(1)} %copy-done.1), kind=kOutput, calls=%fused_computation.56 | convolution fusion | flops 603979776 | bytes 3997696 | tf_op jit(solution)/shard_map/hodw,htcdw->toc/dot_general | solution.py:61
  85.8 2.5 %fusion.19 = f32[9,256,64]{1,2,0:T(8,128)S(1)} fusion(bf16[8,9,64,2,128]{4,2,1,3,0:T(8,128)(2,1)} %fusion.86, bf16[8,256,2,128]{3,1,2,0:T(8,128)(2,1)S(1)} %copy-done.1), kind=kOutput, calls=%fused_computation.54 | convolution fusion | flops 603979776 | bytes 3997696 | tf_op jit(solution)/shard_map/hodw,htcdw->toc/dot_general | solution.py:61
  88.2 1.4 pad_maximum_fusion
  89.7 1.0 convert_element_type.15
  90.7 0.8 copy.73
  91.5 66.3 %reduce-scatter.3.cloned.1.call-done = f32[1,256,2,128]{1,3,2,0:T(8,128)} async-done(((f32[8,256,2,128]{1,3,2,0:T(8,128)}), f32[1,256,2,128]{1,3,2,0:T(8,128)}) %reduce-scatter.3.cloned.1.call-update) | async-done | bytes 262160 | tf_op jit(solution)/shard_map/reduce_scatter | solution.py:75
  157.7 1.0 convert_element_type.14
  158.7 0.8 copy.72
  159.5 12.0 %all-gather.6.cloned.1.call-done = f32[54,256,64]{1,2,0:T(8,128)} async-done(((f32[27,256,64]{1,2,0:T(8,128)}), f32[54,256,64]{1,2,0:T(8,128)}) %all-gather.6.cloned.1.call-update) | async-done | bytes 3538960 | tf_op jit(solution)/shard_map/all_gather | solution.py:113
  171.5 2.5 %reduce_sum.9 = f32[27,256,64]{1,2,0:T(8,128)S(1)} reduce(f32[2,27,256,64]{2,3,1,0:T(8,128)} %bitcast.378, f32[]{:T(128)} %constant.6.clone.1), dimensions={0}, to_apply=%region_2.3 | reduce | flops 442368 | bytes 5308420 | tf_op jit(solution)/shard_map/reduce_sum | solution.py:113
  174.0 1.4 broadcast_multiply_fusion
  (23 shorter events, 1.6 us)
Async XLA Ops:
  7.2 49.5 %all-gather.4.cloned.1.call-start = ((), (), s32[]{:S(2)}) async-start(), calls=%async_computation.3 | async-start | bytes 1179648 | tf_op jit(solution)/shard_map/all_gather | solution.py:81
  8.2 5.3 %collective-permute-start = (bf16[8,64,1,128]{3,1,2,0:T(8,128)(2,1)S(1)}, bf16[8,64,1,128]{3,1,2,0:T(8,128)(2,1)S(1)}, u32[]{:S(2)}, u32[]{:S(2)}) collective-permute-start(bf16[8,64,1,128]{3,1,2,0:T(8,128)(2,1)S(1)} %get-tuple-element.25), channel_id=1, source_target_pairs={{0,1},{2,3},{4,5},{6,7},{8,9},{10,11},{12,13},{14,15},{16,17},{18,... | collective-permute-start | bytes 393224 | tf_op jit(solution)/shard_map/ppermute | solution.py:16
  10.6 3.2 %collective-permute-start.1 = (bf16[8,64,1,128]{3,1,2,0:T(8,128)(2,1)S(1)}, bf16[8,64,1,128]{3,1,2,0:T(8,128)(2,1)S(1)}, u32[]{:S(2)}, u32[]{:S(2)}) collective-permute-start(bf16[8,64,1,128]{3,1,2,0:T(8,128)(2,1)S(1)} %get-tuple-element.26), channel_id=1, source_target_pairs={{1,0},{3,2},{5,4},{7,6},{9,8},{11,10},{13,12},{15,14},{17,16},{19,... | collective-permute-start | bytes 393224 | tf_op jit(solution)/shard_map/ppermute | solution.py:17
  13.5 76.2 %reduce-scatter.5.cloned.1.call-start = ((), (), s32[]{:S(2)}) async-start(), calls=%async_computation.4 | async-start | bytes 786432 | tf_op jit(solution)/shard_map/reduce_scatter | solution.py:108
  16.8 5.2 %copy-start.3 = (bf16[8,64,2,128]{3,2,1,0:T(2,128)(2,1)S(1)}, bf16[8,64,2,128]{3,2,1,0:T(2,128)(2,1)}, u32[]{:S(2)}) copy-start(bf16[8,64,2,128]{3,2,1,0:T(2,128)(2,1)} %param.3) | copy-start | bytes 786436
  58.0 6.3 %collective-permute-start.2 = (bf16[8,256,1,128]{3,1,2,0:T(8,128)(2,1)S(1)}, bf16[8,256,1,128]{3,1,2,0:T(8,128)(2,1)S(1)}, u32[]{:S(2)}, u32[]{:S(2)}) collective-permute-start(bf16[8,256,1,128]{3,1,2,0:T(8,128)(2,1)S(1)} %get-tuple-element.23), channel_id=1, source_target_pairs={{0,1},{2,3},{4,5},{6,7},{8,9},{10,11},{12,13},{14,15},{16,17},{18,... | collective-permute-start | bytes 1572872 | tf_op jit(solution)/shard_map/ppermute | solution.py:16
  59.3 5.0 %collective-permute-start.3 = (bf16[8,256,1,128]{3,1,2,0:T(8,128)(2,1)S(1)}, bf16[8,256,1,128]{3,1,2,0:T(8,128)(2,1)S(1)}, u32[]{:S(2)}, u32[]{:S(2)}) collective-permute-start(bf16[8,256,1,128]{3,1,2,0:T(8,128)(2,1)S(1)} %get-tuple-element.24), channel_id=1, source_target_pairs={{1,0},{3,2},{5,4},{7,6},{9,8},{11,10},{13,12},{15,14},{17,16},{19,... | collective-permute-start | bytes 1572872 | tf_op jit(solution)/shard_map/ppermute | solution.py:17
  61.5 2.8 %copy-start = (bf16[8,256,2,128]{3,1,2,0:T(8,128)(2,1)S(1)}, bf16[8,256,2,128]{3,1,2,0:T(8,128)(2,1)}, u32[]{:S(2)}) copy-start(bf16[8,256,2,128]{3,1,2,0:T(8,128)(2,1)} %all-gather.4.cloned.1.call-done) | copy-start | bytes 3145732
  64.3 1.2 copy-start.2
  71.6 86.1 %reduce-scatter.3.cloned.1.call-start = ((), (), s32[]{:S(2)}) async-start(), calls=%async_computation.2 | async-start | bytes 2359296 | tf_op jit(solution)/shard_map/reduce_scatter | solution.py:75
  76.3 4.5 %copy-start.1 = (bf16[8,256,2,128]{3,1,2,0:T(8,128)(2,1)S(1)}, bf16[8,256,2,128]{3,1,2,0:T(8,128)(2,1)}, u32[]{:S(2)}) copy-start(bf16[8,256,2,128]{3,1,2,0:T(8,128)(2,1)} %all-gather.4.cloned.1.call-done) | copy-start | bytes 3145732
  80.7 90.8 %all-gather.6.cloned.1.call-start = ((), (), s32[]{:S(2)}) async-start(), calls=%async_computation.5 | async-start | bytes 5308416 | tf_op jit(solution)/shard_map/all_gather | solution.py:113
Sparse Core Ops, SparseCore 0:
  13.6 42.9 all-gather.3
  71.7 14.0 reduce-scatter.4
  89.8 67.8 reduce-scatter.2
  159.8 11.6 all-gather.5
